TPU v7x, 32 devices: a whole 2x2x4 slice. The times are simulated.
32 devices in a mesh: aa: 4 (over x, core), ba: 8 (over z, y).
Axes of the slice: x: 2, y: 2, z: 4, core: 2. Of those that a mesh axis runs over, the one named last changes fastest.
Arguments:
- coefficients: float32 [3072, 3072], P('aa', 'ba'), may hold values from -6 to 6
- tile_values: bfloat16 [4, 3, 768, 768], P('aa'), may hold values from -0.125 to 0.125
- tile_cols: int32 [4, 3], P('aa'), may hold values from 0 to 3, as said below
- alpha_energy: float32 [3072], P('aa'), may hold values from -1 to 1
- beta_energy: float32 [3072], P('ba'), may hold values from -1 to 1
Outputs:
- sigma: float32 [3072, 3072], P('aa', 'ba')
Inputs may be any that keep to these rules, and one draw needn't show every extreme that they name: Row r of tile_cols holds r - 1, r and r + 1 taken modulo 4, each once, in some order.
All inputs are finite; a program needn't handle non-finite values.
Results may differ from a plain program's by a relative error of at most 0.0027.
Values may be sent and summed in bfloat16 or wider, within the bound.
A program may use at most 64 MiB of HBM per device.

v0:
```python
import jax
import jax.numpy as jnp
from jax import lax
from jax.sharding import PartitionSpec as P


def passed_along(value, axis, steps):
    count = lax.axis_size(axis)
    pairs = [(source, (source + steps) % count) for source in range(count)]
    return lax.ppermute(value, axis, pairs)


def pick_tile(tile_values, tile_cols, target):
    chosen = jnp.zeros(tile_values.shape[2:], tile_values.dtype)
    for slot in range(tile_values.shape[1]):
        chosen = jnp.where(tile_cols[0, slot] == target, tile_values[0, slot], chosen)
    return chosen


def triple_product(tile_values, tile_cols, own_block, from_above, from_below):
    own_index = lax.axis_index("aa")
    cycle_size = lax.axis_size("aa")
    own_tile = pick_tile(tile_values, tile_cols, own_index)
    above_tile = pick_tile(tile_values, tile_cols, (own_index + 1) % cycle_size)
    below_tile = pick_tile(tile_values, tile_cols, (own_index + cycle_size - 1) % cycle_size)
    summed = jnp.dot(own_tile, own_block, preferred_element_type=jnp.float32)
    summed = summed + jnp.dot(above_tile, from_above, preferred_element_type=jnp.float32)
    return summed + jnp.dot(below_tile, from_below, preferred_element_type=jnp.float32)


def body(coefficients, tile_values, tile_cols, alpha_energy, beta_energy):
    coeff_low = coefficients.astype(jnp.bfloat16)
    landed = lax.all_to_all(
        lax.all_to_all(coeff_low, "ba", split_axis=0, concat_axis=1, tiled=True),
        "aa",
        split_axis=1,
        concat_axis=0,
        tiled=True,
    )
    flipped = landed.T
    alpha_up = passed_along(coeff_low, "aa", -1)
    alpha_down = passed_along(coeff_low, "aa", 1)
    alpha_term = triple_product(tile_values, tile_cols, coeff_low, alpha_up, alpha_down)
    beta_up = passed_along(flipped, "aa", -1)
    beta_down = passed_along(flipped, "aa", 1)
    beta_flip = triple_product(tile_values, tile_cols, flipped, beta_up, beta_down)
    beta_term = lax.all_to_all(
        lax.all_to_all(beta_flip.T, "aa", split_axis=0, concat_axis=1, tiled=True),
        "ba",
        split_axis=1,
        concat_axis=0,
        tiled=True,
    )
    energy = alpha_energy[:, None] + beta_energy[None, :]
    return alpha_term + beta_term + energy * coefficients


def solution(mesh):
    in_specs = (P("aa", "ba"), P("aa", None, None, None), P("aa", None), P("aa"), P("ba"))
    out_specs = P("aa", "ba")
    return jax.shard_map(body, mesh=mesh, in_specs=in_specs, out_specs=out_specs, check_vma=False)
```

profile of v0, /device:TPU:0, one launch (start us, length us, event | category | flops | bytes accessed | tf_op | source)
XLA Modules:
  0.0 119.0 jit_solution(14985577330496708028)
XLA Ops:
  0.0 1.3 %convert_element_type.3 = bf16[768,384]{1,0:T(8,128)(2,1)S(1)} convert(f32[768,384]{1,0:T(8,128)} %param.5) | non-fusion elementwise | flops 294912 | bytes 1769472 | tf_op jit(solution)/shard_map/convert_element_type | solution.py:32
  1.3 0.8 copy-done
  2.2 23.6 %all_to_all.70 = bf16[8,96,384]{2,1,0:T(8,128)(2,1)S(1)} all-to-all(bf16[8,96,384]{2,1,0:T(8,128)(2,1)S(1)} %bitcast.38), channel_id=1, replica_groups=mesh['aa'=4,'ba'=8] {'ba'}, dimensions={0} | all-to-all | bytes 1179648 | tf_op jit(solution)/shard_map/all_to_all | solution.py:34
  25.8 0.2 copy.10
  26.0 0.4 all_to_all.55
  26.4 0.0 copy-start.2
  26.4 0.9 copy.11
  27.3 4.2 %all-to-all-start.1 = ((bf16[96,4,768]{2,0,1:T(8,128)(2,1)}), bf16[96,4,768]{2,0,1:T(8,128)(2,1)}, u32[]{:S(2)}, u32[]{:S(2)}) async-start(bf16[96,4,768]{2,0,1:T(8,128)(2,1)} %copy.11), calls=%async_computation.1 | async-start | bytes 1179648 | tf_op jit(solution)/shard_map/all_to_all | solution.py:33
  31.5 0.6 fusion.10
  37.8 3.3 %all-to-all-done.1 = bf16[96,4,768]{2,0,1:T(8,128)(2,1)} async-done(((bf16[96,4,768]{2,0,1:T(8,128)(2,1)}), bf16[96,4,768]{2,0,1:T(8,128)(2,1)}, u32[]{:S(2)}, u32[]{:S(2)}) %all-to-all-start.1) | async-done | bytes 589856 | tf_op jit(solution)/shard_map/all_to_all | solution.py:33
  41.0 2.3 %select_select_fusion = (bf16[1,1,768,768]{3,2,1,0:T(8,128)(2,1)S(1)}, bf16[1,1,768,768]{3,2,1,0:T(8,128)(2,1)S(1)}, bf16[1,1,768,768]{3,2,1,0:T(8,128)(2,1)S(1)}) fusion(pred[]{:T(512)S(6)} %eq.49, pred[]{:T(512)S(6)} %eq.48, pred[]{:T(512)S(6)} %eq.47, bf16[1,3,768,768]{3,2,1,0:T(8,128)(2,1)} %param.6, pred[]{:T(512)S(6)} %eq.43, pred[]{:T(512)S(6)} %eq.42, ...), kind=kLoop, calls=%fused_computation.14 | loop fusion | flops 5308416 | bytes 7077897 | tf_op jit(solution)/shard_map/jit(_where)/select_n | solution.py:16
  43.4 0.6 collective-permute-start.3
  43.9 1.7 %fusion.6 = f32[768,384]{0,1:T(8,128)S(1)} fusion(bf16[384,768]{1,0:T(8,128)(2,1)} %bitcast.9, bf16[1,1,768,768]{3,2,1,0:T(8,128)(2,1)S(1)} %get-tuple-element.6), kind=kOutput, calls=%fused_computation.10 | convolution fusion | flops 452984832 | bytes 2949120 | tf_op jit(solution)/shard_map/dot_general | solution.py:26
  45.7 6.3 %collective-permute-done.2 = bf16[768,384]{0,1:T(8,128)(2,1)S(1)} collective-permute-done((bf16[768,384]{0,1:T(8,128)(2,1)}, bf16[768,384]{0,1:T(8,128)(2,1)S(1)}, u32[]{:S(2)}, u32[]{:S(2)}) %collective-permute-start.2) | collective-permute-done | bytes 589856 | tf_op jit(solution)/shard_map/ppermute | solution.py:10
  51.9 0.7 convolution_add_fusion.1
  52.6 4.1 %collective-permute-done.3 = bf16[768,384]{0,1:T(8,128)(2,1)S(1)} collective-permute-done((bf16[768,384]{0,1:T(8,128)(2,1)}, bf16[768,384]{0,1:T(8,128)(2,1)S(1)}, u32[]{:S(2)}, u32[]{:S(2)}) %collective-permute-start.3) | collective-permute-done | bytes 589856 | tf_op jit(solution)/shard_map/ppermute | solution.py:10
  56.7 0.7 convolution_add_fusion
  57.4 18.3 %all_to_all.71 = f32[4,96,768]{2,1,0:T(8,128)S(1)} all-to-all(f32[4,96,768]{2,1,0:T(8,128)S(1)} %bitcast.40), channel_id=1, replica_groups=mesh['aa'=4,'ba'=8] {'aa'}, dimensions={0} | all-to-all | bytes 2359296 | tf_op jit(solution)/shard_map/all_to_all | solution.py:48
  75.7 1.8 %copy.12 = f32[96,4,768]{2,1,0:T(4,128)} copy(f32[96,4,768]{2,0,1:T(8,128)S(1)} %bitcast.39) | data formatting | bytes 2359296 | tf_op jit(solution)/shard_map/all_to_all | solution.py:48
  77.4 2.7 %all_to_all.62 = f32[96,8,384]{2,1,0:T(8,128)} reshape(f32[96,4,768]{2,1,0:T(4,128)} %copy.12) | data formatting | bytes 2359296 | tf_op jit(solution)/shard_map/all_to_all | solution.py:47
  80.1 2.5 %copy.13 = f32[96,8,384]{2,0,1:T(8,128)} copy(f32[96,8,384]{2,1,0:T(8,128)} %all_to_all.62) | data formatting | bytes 2359296 | tf_op jit(solution)/shard_map/all_to_all | solution.py:47
  82.6 4.3 %all-to-all-start.3 = ((f32[96,8,384]{2,0,1:T(8,128)}), f32[96,8,384]{2,0,1:T(8,128)}, u32[]{:S(2)}, u32[]{:S(2)}) async-start(f32[96,8,384]{2,0,1:T(8,128)} %copy.13), calls=%async_computation.3 | async-start | bytes 2359296 | tf_op jit(solution)/shard_map/all_to_all | solution.py:47
  86.9 0.1 collective-permute-start
  87.0 0.5 collective-permute-start.1
  87.5 1.8 %fusion.8 = f32[768,384]{1,0:T(8,128)S(1)} fusion(bf16[768,384]{1,0:T(8,128)(2,1)} %copy-done, bf16[1,1,768,768]{3,2,1,0:T(8,128)(2,1)S(1)} %get-tuple-element.6), kind=kOutput, calls=%fused_computation.12 | convolution fusion | flops 452984832 | bytes 2949120 | tf_op jit(solution)/shard_map/dot_general | solution.py:26
  89.3 0.0 copy-start.1
  89.3 0.0 copy-start.3
  89.3 11.2 %collective-permute-done = bf16[768,384]{1,0:T(8,128)(2,1)S(1)} collective-permute-done((bf16[768,384]{1,0:T(8,128)(2,1)}, bf16[768,384]{1,0:T(8,128)(2,1)S(1)}, u32[]{:S(2)}, u32[]{:S(2)}) %collective-permute-start) | collective-permute-done | bytes 589856 | tf_op jit(solution)/shard_map/ppermute | solution.py:10
  100.5 1.8 %convolution_add_fusion.3 = f32[768,384]{1,0:T(8,128)} fusion(f32[768,384]{1,0:T(8,128)S(1)} %fusion.8, bf16[768,384]{1,0:T(8,128)(2,1)S(1)} %collective-permute-done, bf16[1,1,768,768]{3,2,1,0:T(8,128)(2,1)S(1)} %get-tuple-element.7), kind=kOutput, calls=%fused_computation.5 | convolution fusion | flops 453279744 | bytes 4128768 | tf_op jit(solution)/shard_map/dot_general | solution.py:27
  102.3 0.2 collective-permute-done.1
  102.5 12.8 %all-to-all-done.3 = f32[96,8,384]{2,0,1:T(8,128)} async-done(((f32[96,8,384]{2,0,1:T(8,128)}), f32[96,8,384]{2,0,1:T(8,128)}, u32[]{:S(2)}, u32[]{:S(2)}) %all-to-all-start.3) | async-done | bytes 1179680 | tf_op jit(solution)/shard_map/all_to_all | solution.py:47
  115.4 3.6 %fusion.1 = f32[768,384]{1,0:T(8,128)} fusion(f32[768,384]{1,0:T(8,128)} %bitcast.17, f32[768,384]{1,0:T(8,128)} %convolution_add_fusion.3, bf16[768,384]{1,0:T(8,128)(2,1)} %collective-permute-done.1, bf16[1,1,768,768]{3,2,1,0:T(8,128)(2,1)S(1)} %get-tuple-element.5, f32[768,384]{1,0:T(8,128)S(1)} %copy-done.1, f32[384]{0:T(512)S(1)} %copy-done.4, ...), kind=kOutput, calls=%fused_computation.4 | convolution fusion | flops 454459392 | bytes 6492672 | tf_op jit(solution)/shard_map/dot_general | solution.py:28
  (7 shorter events, 0.0 us)
Async XLA Ops:
  1.3 0.8 copy-start
  26.4 5.1 %copy-start.2 = (s32[1,3]{1,0:T(1,128)S(1)}, s32[1,3]{1,0:T(1,128)}, u32[]{:S(2)}) copy-start(s32[1,3]{1,0:T(1,128)} %param.7) | copy-start | bytes 40
  27.3 13.8 %all-to-all-start.1 = ((bf16[96,4,768]{2,0,1:T(8,128)(2,1)}), bf16[96,4,768]{2,0,1:T(8,128)(2,1)}, u32[]{:S(2)}, u32[]{:S(2)}) async-start(bf16[96,4,768]{2,0,1:T(8,128)(2,1)} %copy.11), calls=%async_computation.1 | async-start | bytes 1179648 | tf_op jit(solution)/shard_map/all_to_all | solution.py:33
  41.0 10.9 %collective-permute-start.2 = (bf16[768,384]{0,1:T(8,128)(2,1)}, bf16[768,384]{0,1:T(8,128)(2,1)S(1)}, u32[]{:S(2)}, u32[]{:S(2)}) collective-permute-start(bf16[768,384]{0,1:T(8,128)(2,1)} %bitcast.11), channel_id=1, source_target_pairs={{0,24},{8,0},{16,8},{24,16},{1,25},{9,1},{17,9},{25,17},{2,26},{10... | collective-permute-start | bytes 1769480 | tf_op jit(solution)/shard_map/ppermute | solution.py:10
  43.4 13.3 %collective-permute-start.3 = (bf16[768,384]{0,1:T(8,128)(2,1)}, bf16[768,384]{0,1:T(8,128)(2,1)S(1)}, u32[]{:S(2)}, u32[]{:S(2)}) collective-permute-start(bf16[768,384]{0,1:T(8,128)(2,1)} %bitcast.11), channel_id=1, source_target_pairs={{0,8},{8,16},{16,24},{24,0},{1,9},{9,17},{17,25},{25,1},{2,10},{10... | collective-permute-start | bytes 1769480 | tf_op jit(solution)/shard_map/ppermute | solution.py:10
  82.6 32.8 %all-to-all-start.3 = ((f32[96,8,384]{2,0,1:T(8,128)}), f32[96,8,384]{2,0,1:T(8,128)}, u32[]{:S(2)}, u32[]{:S(2)}) async-start(f32[96,8,384]{2,0,1:T(8,128)} %copy.13), calls=%async_computation.3 | async-start | bytes 2359296 | tf_op jit(solution)/shard_map/all_to_all | solution.py:47
  86.9 13.6 %collective-permute-start = (bf16[768,384]{1,0:T(8,128)(2,1)}, bf16[768,384]{1,0:T(8,128)(2,1)S(1)}, u32[]{:S(2)}, u32[]{:S(2)}) collective-permute-start(bf16[768,384]{1,0:T(8,128)(2,1)} %copy-done), channel_id=1, source_target_pairs={{0,24},{8,0},{16,8},{24,16},{1,25},{9,1},{17,9},{25,17},{2,26},{10... | collective-permute-start | bytes 1769480 | tf_op jit(solution)/shard_map/ppermute | solution.py:10
  87.0 15.6 %collective-permute-start.1 = (bf16[768,384]{1,0:T(8,128)(2,1)}, bf16[768,384]{1,0:T(8,128)(2,1)}, u32[]{:S(2)}, u32[]{:S(2)}) collective-permute-start(bf16[768,384]{1,0:T(8,128)(2,1)} %copy-done), channel_id=1, source_target_pairs={{0,8},{8,16},{16,24},{24,0},{1,9},{9,17},{17,25},{25,1},{2,10},{10... | collective-permute-start | bytes 1769480 | tf_op jit(solution)/shard_map/ppermute | solution.py:10
  89.3 26.1 %copy-start.1 = (f32[768,384]{1,0:T(8,128)S(1)}, f32[768,384]{1,0:T(8,128)}, u32[]{:S(2)}) copy-start(f32[768,384]{1,0:T(8,128)} %param.5) | copy-start | bytes 3538948
  89.3 26.1 %copy-start.3 = (f32[768]{0:T(1024)S(1)}, f32[768]{0:T(1024)}, u32[]{:S(2)}) copy-start(f32[768]{0:T(1024)} %param.8) | copy-start | bytes 9220
  89.3 26.1 %copy-start.4 = (f32[384]{0:T(512)S(1)}, f32[384]{0:T(512)}, u32[]{:S(2)}) copy-start(f32[384]{0:T(512)} %param.9) | copy-start | bytes 4612
where the time goes:
time: 120 us; the launch traced here: 119 us
  blocking collectives  41.9 us (35%)
  waiting for transfers between devices  37.9 us (32%)
  matrix products  10.3 us (9%)
  local copies, waits for them, and re-layouts  9.9 us (8%)
  starting transfers between devices  9.54 us (8%)
  between operations  5.8 us (5%)
  other arithmetic  3.67 us (3%)
    all_to_all x1, blocking collectives, body(): lax.all_to_all(coeff_low, 'ba', split_axis=0, concat_axis=1, tiled=True)  23.6 us
    ppermute x4, waiting for transfers between devices, passed_along(): return lax.ppermute(value, axis, pairs)  21.8 us
    all_to_all x1, blocking collectives, body(): lax.all_to_all(beta_flip.T, 'aa', split_axis=0, concat_axis=1, tiled=True)  18.3 us
    all_to_all x1, waiting for transfers between devices, body(): lax.all_to_all(lax.all_to_all(beta_flip.T, 'aa', split_axis=0, concat_axi...  12.8 us
    all_to_all x2, local copies, waits for them, and re-layouts, body(): lax.all_to_all(lax.all_to_all(beta_flip.T, 'aa', split_axis=0, concat_axi...  5.2 us
    dot_general x2, matrix products, triple_product(): jnp.dot(below_tile, from_below, preferred_element_type=jnp.float32)  4.27 us
    all_to_all x1, starting transfers between devices, body(): lax.all_to_all(lax.all_to_all(beta_flip.T, 'aa', split_axis=0, concat_axi...  4.26 us
    all_to_all x1, starting transfers between devices, body(): lax.all_to_all(lax.all_to_all(coeff_low, 'ba', split_axis=0, concat_axis=...  4.16 us
  transfers between devices with their start and end apart: 6, of which 6 were waited for; matrix products, arithmetic and copies ran while one was open for 8% of the time, Pallas kernels for 0%

commit v1 on v0

v1 whole, which is shorter than its diff:
```python
import functools

import jax
import jax.numpy as jnp
from jax import lax
from jax.experimental import pallas as pl
from jax.experimental.pallas import tpu as pltpu
from jax.sharding import PartitionSpec as P

MESH = pl.DeviceIdType.MESH


def kernel(count, c_ref, h_hbm, cols_ref, ae_ref, be_ref, out_ref,
           ha, hb, c16, nb, g, rs, rr, own,
           load_sem, y_send, y_recv, z_send, z_recv, a_send, a_recv,
           h_send, h_recv, w_send, f_send, r_send, r_recv):
    a = lax.axis_index("aa")
    b = lax.axis_index("ba")
    side = b % 2
    core = a % 2
    block = b // 2
    partner = b + 1 - 2 * side
    sibling = a + 1 - 2 * core
    blocks = 2 * count
    rows, width = c_ref.shape
    half = rows // 2
    quarter = rows // 4
    up_a, down_a = (a + 1) % count, (a + count - 1) % count
    up_b, down_b = (b + 2) % blocks, (b + blocks - 2) % blocks

    loads = [pltpu.make_async_copy(h_hbm.at[0, s], ha.at[s], load_sem.at[s]) for s in range(3)]
    for load in loads:
        load.start()

    barrier = pltpu.get_barrier_semaphore()
    greeted = [((a + d) % count, b) for d in range(1, count)]
    greeted += [(a, partner), (a, up_b), (a, down_b)]
    for device in greeted:
        pl.semaphore_signal(barrier, inc=1, device_id=device, device_id_type=MESH)

    c16[...] = c_ref[...].astype(jnp.bfloat16)
    g[1, side] = c16[pl.ds(pl.multiple_of(side * half, half), half), :]

    def remote(src, dst, send, recv, device):
        return pltpu.make_async_remote_copy(
            src_ref=src, dst_ref=dst, send_sem=send, recv_sem=recv,
            device_id=device, device_id_type=MESH)

    y_copy = remote(c16.at[pl.ds(pl.multiple_of((1 - side) * half, half), half)],
                    g.at[1, side], y_send.at[0], y_recv.at[0], (a, partner))
    y_wait = remote(g.at[1, 1 - side], g.at[1, 1 - side], y_send.at[0], y_recv.at[0], (a, partner))

    def z_copies(which, column):
        return [remote(g.at[1, column], g.at[0, column], z_send.at[0, which], z_recv.at[0, which], (a, up_b)),
                remote(g.at[1, column], g.at[2, column], z_send.at[1, which], z_recv.at[1, which], (a, down_b))]

    a_copies = [remote(c16, nb.at[0], a_send.at[0], a_recv.at[0], (up_a, b)),
                remote(c16, nb.at[1], a_send.at[1], a_recv.at[1], (down_a, b))]

    pl.semaphore_wait(barrier, len(greeted))
    y_copy.start()
    z_own = z_copies(0, side)
    for copy in z_own:
        copy.start()

    for load in loads:
        load.wait()
    found = [cols_ref[0, s] for s in range(3)]

    def slot_of(offset):
        target = (a + offset + count) % count
        return jnp.where(found[0] == target, 0, jnp.where(found[1] == target, 1, 2))

    slots = [slot_of(offset) for offset in (-1, 0, 1)]

    def piece(s, q):
        return hb.at[s, pl.ds(pl.multiple_of(q * quarter, quarter), quarter)]

    source = a == block
    near = a // 2 == block // 2
    pairs = count // 2

    def spread(s, d, c):
        pair = (a // 2 + d) % pairs
        q = 2 * side + c
        return remote(piece(s, q), piece(s, q), h_send.at[s, d - 1, c], h_recv.at[s, q], (2 * pair + c, b))

    def whole(s):
        return remote(hb.at[s], hb.at[s], w_send.at[s], h_recv.at[s, 0], (sibling, b))

    def forward(s, q, device, index):
        return remote(piece(s, q), piece(s, q), f_send.at[s, index], h_recv.at[s, q], device)

    @pl.when(source)
    def _():
        for s in range(3):
            @pl.loop(0, 4)
            def _(i):
                at = pl.ds(pl.multiple_of(i * quarter, quarter), quarter)
                hb[s, at, :] = ha[slots[s], at, :]
            for d in range(1, pairs):
                for c in range(2):
                    spread(s, d, c).start()
            whole(s).start()

    y_wait.wait_recv()
    z_far = z_copies(1, 1 - side)
    for copy in z_far:
        copy.start()
    for copy in a_copies:
        copy.start()

    tile = rows // 3

    @pl.loop(0, 3)
    def _(i):
        at = pl.ds(pl.multiple_of(i * tile, tile), tile)
        column = jnp.transpose(jnp.broadcast_to(ae_ref[0:1, at], (128, tile)))[:, 0:1]
        energy = column + be_ref[...]
        out_ref[at, :] = energy * c_ref[at, :] + jnp.dot(
            ha[slots[1], at, :], c16[...], preferred_element_type=jnp.float32)

    mine, theirs = 2 * side + core, 2 * (1 - side) + core

    @pl.when(jnp.logical_not(near))
    def _():
        for s in range(3):
            forward(s, mine, (a, partner), 0).wait_recv()
            forward(s, mine, (a, partner), 0).start()
            forward(s, mine, (sibling, b), 1).start()
        for s in range(3):
            forward(s, theirs, (sibling, b), 2).wait_recv()
            forward(s, theirs, (sibling, b), 2).start()
        for s in range(3):
            forward(s, 2 * side + 1 - core, (sibling, b), 1).wait_recv()
            forward(s, 2 * (1 - side) + 1 - core, (sibling, b), 1).wait_recv()

    @pl.when(jnp.logical_and(near, jnp.logical_not(source)))
    def _():
        for s in range(3):
            whole(s).wait_recv()

    for copy in z_own + z_far:
        copy.wait_recv()

    def beta(j, start, size):
        at = pl.ds(pl.multiple_of(start, 128), size)
        total = None
        for k in (1, 0, 2):
            left = jnp.concatenate([g[k, 0], g[k, 1]], axis=1)
            product = lax.dot_general(left, hb[k, at, :], (((1,), (1,)), ((), ())),
                                      preferred_element_type=jnp.float32)
            total = product if total is None else total + product
        return total

    rs[...] = beta(0, (1 - side) * width, width).astype(jnp.bfloat16)
    r_copy = remote(rs, rr, r_send.at[0], r_recv.at[0], (a, partner))
    r_copy.start()
    at_own = pl.ds(pl.multiple_of(side * half, half), half)
    at_other = pl.ds(pl.multiple_of((1 - side) * half, half), half)
    out_ref[at_own, :] += beta(0, side * width, width)

    for copy in a_copies:
        copy.wait_recv()

    @pl.loop(0, 3)
    def _(i):
        at = pl.ds(pl.multiple_of(i * tile, tile), tile)
        out_ref[at, :] += jnp.dot(
            ha[slots[0], at, :], nb[0], preferred_element_type=jnp.float32
        ) + jnp.dot(ha[slots[2], at, :], nb[1], preferred_element_type=jnp.float32)

    r_copy.wait_recv()
    out_ref[at_other, :] += rr[...].astype(jnp.float32)

    for copy in z_own + z_far + a_copies + [y_copy, r_copy]:
        copy.wait_send()

    @pl.when(source)
    def _():
        for s in range(3):
            for d in range(1, pairs):
                for c in range(2):
                    spread(s, d, c).wait_send()
            whole(s).wait_send()

    @pl.when(jnp.logical_not(near))
    def _():
        for s in range(3):
            forward(s, mine, (a, partner), 0).wait_send()
            forward(s, mine, (sibling, b), 1).wait_send()
            forward(s, theirs, (sibling, b), 2).wait_send()


def body(count, coefficients, tile_values, tile_cols, alpha_energy, beta_energy):
    rows, width = coefficients.shape
    half = rows // 2
    low = jnp.bfloat16
    dma = pltpu.SemaphoreType.DMA
    vmem = pl.BlockSpec(memory_space=pltpu.VMEM)
    return pl.pallas_call(
        functools.partial(kernel, count),
        out_shape=jax.ShapeDtypeStruct((rows, width), jnp.float32),
        in_specs=[vmem, pl.BlockSpec(memory_space=pl.ANY),
                  pl.BlockSpec(memory_space=pltpu.SMEM), vmem, vmem],
        out_specs=vmem,
        scratch_shapes=[
            pltpu.VMEM((3, rows, rows), low),
            pltpu.VMEM((3, rows, rows), low),
            pltpu.VMEM((rows, width), low),
            pltpu.VMEM((2, rows, width), low),
            pltpu.VMEM((3, 2, half, width), low),
            pltpu.VMEM((half, width), low),
            pltpu.VMEM((half, width), low),
            pltpu.VMEM((8, 128), jnp.float32),
            dma((3,)), dma((1,)), dma((1,)), dma((2, 2)), dma((2, 2)), dma((2,)), dma((2,)),
            dma((3, count // 2 - 1, 2)), dma((3, 4)), dma((3,)), dma((3, 3)), dma((1,)), dma((1,)),
        ],
        compiler_params=pltpu.CompilerParams(
            collective_id=0, has_side_effects=True, vmem_limit_bytes=48 * 1024 * 1024),
        cost_estimate=pl.CostEstimate(
            flops=12 * rows * rows * width, bytes_accessed=8 * rows * rows, transcendentals=0),
    )(coefficients, tile_values, tile_cols,
      alpha_energy.reshape(1, rows), beta_energy.reshape(1, width))


def solution(mesh):
    in_specs = (P("aa", "ba"), P("aa", None, None, None), P("aa", None), P("aa"), P("ba"))
    return jax.shard_map(functools.partial(body, mesh.shape["aa"]), mesh=mesh,
                         in_specs=in_specs, out_specs=P("aa", "ba"), check_vma=False)
```

time: 120 us -> 54.3 us (0.45)
  the two profiles are of different devices: /device:TPU:0 before, /device:TPU:2 now
where the time goes in v1:
time: 54.3 us; the launch traced here: 54.1 us
  Pallas kernels  47.7 us (88%)
  local copies, waits for them, and re-layouts  6.31 us (12%)
    pallas_call x1, Pallas kernels, body(): pl.pallas_call(functools.partial(kernel, count), out_shape=jax.ShapeDtype...  47.7 us
    unnamed x7, local copies, waits for them, and re-layouts  4.94 us

profile of v1, /device:TPU:2, one launch (start us, length us, event | category | flops | bytes accessed | tf_op | source)
XLA Modules:
  0.0 54.1 jit_solution(10447901324848556788)
XLA Ops:
  0.0 0.7 %reshape.7.be_ref = f32[1,384]{1,0:T(1,128)S(1)} reshape(f32[384]{0:T(512)} %param.9) | data formatting | bytes 3072 | tf_op jit(solution)/shard_map/reshape | solution.py:224
  0.7 0.7 %reshape.6.ae_ref = f32[1,768]{1,0:T(1,128)S(1)} reshape(f32[768]{0:T(1024)} %param.8) | data formatting | bytes 6144 | tf_op jit(solution)/shard_map/reshape | solution.py:224
  1.4 0.0 copy-start
  1.4 2.0 %copy-done = bf16[1,3,768,768]{3,2,1,0:T(8,128)(2,1)S(1)} copy-done((bf16[1,3,768,768]{3,2,1,0:T(8,128)(2,1)S(1)}, bf16[1,3,768,768]{3,2,1,0:T(8,128)(2,1)}, u32[]{:S(2)}) %copy-start) | copy-done | bytes 3538968
  3.4 0.0 copy-start.1
  3.4 1.3 %copy-done.1 = f32[768,384]{1,0:T(8,128)S(1)} copy-done((f32[768,384]{1,0:T(8,128)S(1)}, f32[768,384]{1,0:T(8,128)}, u32[]{:S(2)}) %copy-start.1) | copy-done | bytes 1179672
  4.6 0.0 copy-start.2
  4.6 0.7 %copy-done.2 = s32[1,3]{1,0:T(1,128)S(1)} copy-done((s32[1,3]{1,0:T(1,128)S(1)}, s32[1,3]{1,0:T(1,128)}, u32[]{:S(2)}) %copy-start.2) | copy-done | bytes 36
  5.3 47.7 %shard_map.55 = f32[768,384]{1,0:T(8,128)S(1)} custom-call(f32[768,384]{1,0:T(8,128)S(1)} %copy-done.1, bf16[1,3,768,768]{3,2,1,0:T(8,128)(2,1)S(1)} %copy-done, s32[1,3]{1,0:T(1,128)S(1)} %copy-done.2, f32[1,768]{1,0:T(1,128)S(1)} %reshape.6.ae_ref, f32[1,384]{1,0:T(1,128)S(1)} %reshape.7.be_ref), custom_call_target="tpu_custom_call" | custom-call | flops 2717908992 | bytes 4718592 | tf_op jit(solution)/shard_map/pallas_call | solution.py:201
  53.0 1.0 %copy.7 = f32[768,384]{1,0:T(8,128)} copy(f32[768,384]{1,0:T(8,128)S(1)} %shard_map.55) | data formatting | bytes 2359296
Async XLA Ops:
  1.4 2.0 %copy-start = (bf16[1,3,768,768]{3,2,1,0:T(8,128)(2,1)S(1)}, bf16[1,3,768,768]{3,2,1,0:T(8,128)(2,1)}, u32[]{:S(2)}) copy-start(bf16[1,3,768,768]{3,2,1,0:T(8,128)(2,1)} %h_hbm.1) | copy-start | bytes 10616836
  3.4 1.3 %copy-start.1 = (f32[768,384]{1,0:T(8,128)S(1)}, f32[768,384]{1,0:T(8,128)}, u32[]{:S(2)}) copy-start(f32[768,384]{1,0:T(8,128)} %c_ref.1) | copy-start | bytes 3538948
  4.6 0.7 %copy-start.2 = (s32[1,3]{1,0:T(1,128)S(1)}, s32[1,3]{1,0:T(1,128)}, u32[]{:S(2)}) copy-start(s32[1,3]{1,0:T(1,128)} %cols_ref.1) | copy-start | bytes 40

commit v2 on v1

--- a/solution.py
+++ b/solution.py
@@ -10,8 +10,8 @@
 MESH = pl.DeviceIdType.MESH
 
 
-def kernel(count, c_ref, h_hbm, cols_ref, ae_ref, be_ref, out_ref,
-           ha, hb, c16, nb, g, rs, rr, own,
+def kernel(count, c_hbm, h_hbm, cols_hbm, ae_ref, be_ref, out_ref,
+           c_ref, cols_ref, ha, hb, c16, nb, g, rs, rr,
            load_sem, y_send, y_recv, z_send, z_recv, a_send, a_recv,
            h_send, h_recv, w_send, f_send, r_send, r_recv):
     a = lax.axis_index("aa")
@@ -28,7 +28,10 @@
     up_a, down_a = (a + 1) % count, (a + count - 1) % count
     up_b, down_b = (b + 2) % blocks, (b + blocks - 2) % blocks
 
+    first = pltpu.make_async_copy(c_hbm, c_ref, load_sem.at[3])
+    first.start()
     loads = [pltpu.make_async_copy(h_hbm.at[0, s], ha.at[s], load_sem.at[s]) for s in range(3)]
+    loads.append(pltpu.make_async_copy(cols_hbm, cols_ref, load_sem.at[4]))
     for load in loads:
         load.start()
 
@@ -38,6 +41,7 @@
     for device in greeted:
         pl.semaphore_signal(barrier, inc=1, device_id=device, device_id_type=MESH)
 
+    first.wait()
     c16[...] = c_ref[...].astype(jnp.bfloat16)
     g[1, side] = c16[pl.ds(pl.multiple_of(side * half, half), half), :]
 
@@ -56,6 +60,15 @@
 
     a_copies = [remote(c16, nb.at[0], a_send.at[0], a_recv.at[0], (up_a, b)),
                 remote(c16, nb.at[1], a_send.at[1], a_recv.at[1], (down_a, b))]
+
+    def start_cross():
+        @pl.when(core == 1)
+        def _():
+            a_copies[0].start()
+
+        @pl.when(core == 0)
+        def _():
+            a_copies[1].start()
 
     pl.semaphore_wait(barrier, len(greeted))
     y_copy.start()
@@ -63,6 +76,14 @@
     for copy in z_own:
         copy.start()
 
+    @pl.when(core == 0)
+    def _():
+        a_copies[0].start()
+
+    @pl.when(core == 1)
+    def _():
+        a_copies[1].start()
+
     for load in loads:
         load.wait()
     found = [cols_ref[0, s] for s in range(3)]
@@ -82,7 +103,7 @@
 
     def spread(s, d, c):
         pair = (a // 2 + d) % pairs
-        q = 2 * side + c
+        q = 2 * (1 - side) + c
         return remote(piece(s, q), piece(s, q), h_send.at[s, d - 1, c], h_recv.at[s, q], (2 * pair + c, b))
 
     def whole(s):
@@ -107,8 +128,9 @@
     z_far = z_copies(1, 1 - side)
     for copy in z_far:
         copy.start()
-    for copy in a_copies:
-        copy.start()
+    @pl.when(jnp.logical_not(near))
+    def _():
+        start_cross()
 
     tile = rows // 3
 
@@ -120,7 +142,7 @@
         out_ref[at, :] = energy * c_ref[at, :] + jnp.dot(
             ha[slots[1], at, :], c16[...], preferred_element_type=jnp.float32)
 
-    mine, theirs = 2 * side + core, 2 * (1 - side) + core
+    mine, theirs = 2 * (1 - side) + core, 2 * side + core
 
     @pl.when(jnp.logical_not(near))
     def _():
@@ -132,15 +154,29 @@
             forward(s, theirs, (sibling, b), 2).wait_recv()
             forward(s, theirs, (sibling, b), 2).start()
         for s in range(3):
+            forward(s, 2 * (1 - side) + 1 - core, (sibling, b), 1).wait_recv()
             forward(s, 2 * side + 1 - core, (sibling, b), 1).wait_recv()
-            forward(s, 2 * (1 - side) + 1 - core, (sibling, b), 1).wait_recv()
 
     @pl.when(jnp.logical_and(near, jnp.logical_not(source)))
     def _():
         for s in range(3):
             whole(s).wait_recv()
 
-    for copy in z_own + z_far:
+    for copy in z_own:
+        copy.wait_recv()
+
+    @pl.when(source)
+    def _():
+        for s in range(3):
+            for d in range(1, pairs):
+                for c in range(2):
+                    spread(s, d, c).wait_send()
+
+    @pl.when(near)
+    def _():
+        start_cross()
+
+    for copy in z_far:
         copy.wait_recv()
 
     def beta(j, start, size):
@@ -179,9 +215,6 @@
     @pl.when(source)
     def _():
         for s in range(3):
-            for d in range(1, pairs):
-                for c in range(2):
-                    spread(s, d, c).wait_send()
             whole(s).wait_send()
 
     @pl.when(jnp.logical_not(near))
@@ -197,14 +230,16 @@
     half = rows // 2
     low = jnp.bfloat16
     dma = pltpu.SemaphoreType.DMA
+    hbm = pl.BlockSpec(memory_space=pltpu.HBM)
     vmem = pl.BlockSpec(memory_space=pltpu.VMEM)
     return pl.pallas_call(
         functools.partial(kernel, count),
         out_shape=jax.ShapeDtypeStruct((rows, width), jnp.float32),
-        in_specs=[vmem, pl.BlockSpec(memory_space=pl.ANY),
-                  pl.BlockSpec(memory_space=pltpu.SMEM), vmem, vmem],
+        in_specs=[hbm, hbm, hbm, vmem, vmem],
         out_specs=vmem,
         scratch_shapes=[
+            pltpu.VMEM((rows, width), jnp.float32),
+            pltpu.SMEM(tile_cols.shape, jnp.int32),
             pltpu.VMEM((3, rows, rows), low),
             pltpu.VMEM((3, rows, rows), low),
             pltpu.VMEM((rows, width), low),
@@ -212,12 +247,11 @@
             pltpu.VMEM((3, 2, half, width), low),
             pltpu.VMEM((half, width), low),
             pltpu.VMEM((half, width), low),
-            pltpu.VMEM((8, 128), jnp.float32),
-            dma((3,)), dma((1,)), dma((1,)), dma((2, 2)), dma((2, 2)), dma((2,)), dma((2,)),
+            dma((5,)), dma((1,)), dma((1,)), dma((2, 2)), dma((2, 2)), dma((2,)), dma((2,)),
             dma((3, count // 2 - 1, 2)), dma((3, 4)), dma((3,)), dma((3, 3)), dma((1,)), dma((1,)),
         ],
         compiler_params=pltpu.CompilerParams(
-            collective_id=0, has_side_effects=True, vmem_limit_bytes=48 * 1024 * 1024),
+            collective_id=0, has_side_effects=True, vmem_limit_bytes=63 * 1024 * 1024),
         cost_estimate=pl.CostEstimate(
             flops=12 * rows * rows * width, bytes_accessed=8 * rows * rows, transcendentals=0),
     )(coefficients, tile_values, tile_cols,

time: 54.3 us -> 52.7 us (0.971)
  local copies, waits for them, and re-layouts: 6.31 us -> 4.88 us
    unnamed x7 -> x1, local copies, waits for them, and re-layouts: 4.94 us -> 2.36 us
    reshape x1, local copies, waits for them, and re-layouts: 0.69 us -> 1.27 us  [body(): alpha_energy.reshape(1, rows)]
    reshape x1, local copies, waits for them, and re-layouts: 0.68 us -> 1.25 us  [body(): beta_energy.reshape(1, width)]
where the time goes in v2:
time: 52.7 us; the launch traced here: 52.5 us
  Pallas kernels  47.6 us (90%)
  local copies, waits for them, and re-layouts  4.88 us (9%)
    pallas_call x1, Pallas kernels, body(): pl.pallas_call(functools.partial(kernel, count), out_shape=jax.ShapeDtype...  47.6 us
    unnamed x1, local copies, waits for them, and re-layouts  2.36 us
    reshape x1, local copies, waits for them, and re-layouts, body(): alpha_energy.reshape(1, rows)  1.27 us
    reshape x1, local copies, waits for them, and re-layouts, body(): beta_energy.reshape(1, width)  1.25 us

profile of v2, /device:TPU:2, one launch (start us, length us, event | category | flops | bytes accessed | tf_op | source)
XLA Modules:
  0.0 52.5 jit_solution(3765665650137417617)
XLA Ops:
  0.0 1.3 %reshape.7.be_ref = f32[1,384]{1,0:T(1,128)} reshape(f32[384]{0:T(512)} %param.9) | data formatting | bytes 3072 | tf_op jit(solution)/shard_map/reshape | solution.py:258
  1.3 1.3 %reshape.6.ae_ref = f32[1,768]{1,0:T(1,128)} reshape(f32[768]{0:T(1024)} %param.8) | data formatting | bytes 6144 | tf_op jit(solution)/shard_map/reshape | solution.py:258
  2.5 47.6 %shard_map.55 = f32[768,384]{1,0:T(8,128)} custom-call(f32[768,384]{1,0:T(8,128)} %c_hbm.1, bf16[1,3,768,768]{3,2,1,0:T(8,128)(2,1)} %h_hbm.1, s32[1,3]{1,0:T(1,128)} %cols_hbm.1, f32[1,768]{1,0:T(1,128)} %reshape.6.ae_ref, f32[1,384]{1,0:T(1,128)} %reshape.7.be_ref), custom_call_target="tpu_custom_call" | custom-call | flops 2717908992 | bytes 4718592 | tf_op jit(solution)/shard_map/pallas_call | solution.py:235
  50.1 2.4 %copy.7 = f32[768,384]{1,0:T(8,128)} copy(f32[768,384]{1,0:T(8,128)} %shard_map.55) | data formatting | bytes 2359296

commit v3 on v2

--- a/solution.py
+++ b/solution.py
@@ -10,7 +10,7 @@
 MESH = pl.DeviceIdType.MESH
 
 
-def kernel(count, c_hbm, h_hbm, cols_hbm, ae_ref, be_ref, out_ref,
+def kernel(count, c_hbm, h_hbm, cols_hbm, out_ref,
            c_ref, cols_ref, ha, hb, c16, nb, g, rs, rr,
            load_sem, y_send, y_recv, z_send, z_recv, a_send, a_recv,
            h_send, h_recv, w_send, f_send, r_send, r_recv):
@@ -132,16 +132,6 @@
     def _():
         start_cross()
 
-    tile = rows // 3
-
-    @pl.loop(0, 3)
-    def _(i):
-        at = pl.ds(pl.multiple_of(i * tile, tile), tile)
-        column = jnp.transpose(jnp.broadcast_to(ae_ref[0:1, at], (128, tile)))[:, 0:1]
-        energy = column + be_ref[...]
-        out_ref[at, :] = energy * c_ref[at, :] + jnp.dot(
-            ha[slots[1], at, :], c16[...], preferred_element_type=jnp.float32)
-
     mine, theirs = 2 * (1 - side) + core, 2 * side + core
 
     @pl.when(jnp.logical_not(near))
@@ -194,15 +184,20 @@
     r_copy.start()
     at_own = pl.ds(pl.multiple_of(side * half, half), half)
     at_other = pl.ds(pl.multiple_of((1 - side) * half, half), half)
-    out_ref[at_own, :] += beta(0, side * width, width)
+    out_ref[at_other, :] = jnp.zeros((half, width), jnp.float32)
+    out_ref[at_own, :] = beta(0, side * width, width)
 
     for copy in a_copies:
         copy.wait_recv()
+
+    tile = rows // 3
 
     @pl.loop(0, 3)
     def _(i):
         at = pl.ds(pl.multiple_of(i * tile, tile), tile)
         out_ref[at, :] += jnp.dot(
+            ha[slots[1], at, :], c16[...], preferred_element_type=jnp.float32
+        ) + jnp.dot(
             ha[slots[0], at, :], nb[0], preferred_element_type=jnp.float32
         ) + jnp.dot(ha[slots[2], at, :], nb[1], preferred_element_type=jnp.float32)
 
@@ -232,10 +227,10 @@
     dma = pltpu.SemaphoreType.DMA
     hbm = pl.BlockSpec(memory_space=pltpu.HBM)
     vmem = pl.BlockSpec(memory_space=pltpu.VMEM)
-    return pl.pallas_call(
+    coupled = pl.pallas_call(
         functools.partial(kernel, count),
         out_shape=jax.ShapeDtypeStruct((rows, width), jnp.float32),
-        in_specs=[hbm, hbm, hbm, vmem, vmem],
+        in_specs=[hbm, hbm, hbm],
         out_specs=vmem,
         scratch_shapes=[
             pltpu.VMEM((rows, width), jnp.float32),
@@ -254,8 +249,8 @@
             collective_id=0, has_side_effects=True, vmem_limit_bytes=63 * 1024 * 1024),
         cost_estimate=pl.CostEstimate(
             flops=12 * rows * rows * width, bytes_accessed=8 * rows * rows, transcendentals=0),
-    )(coefficients, tile_values, tile_cols,
-      alpha_energy.reshape(1, rows), beta_energy.reshape(1, width))
+    )(coefficients, tile_values, tile_cols)
+    return coupled + (alpha_energy[:, None] + beta_energy[None, :]) * coefficients
 
 
 def solution(mesh):

time: 52.7 us -> 50 us (0.949)
  local copies, waits for them, and re-layouts: 4.88 us -> 0.01 us
  other arithmetic: 0 us -> 2.85 us
  Pallas kernels: 47.6 us -> 46.9 us
    add x0 -> x1, other arithmetic: none -> 2.85 us  [body(): coupled + (alpha_energy[:, None] + beta_energy[None, :]) * coefficients]
    reshape x2 -> x0, local copies, waits for them, and re-layouts: 2.52 us -> none  [the longest x1 1.27 us: body(): alpha_energy.reshape(1, rows)]
    unnamed x1 -> x4, local copies, waits for them, and re-layouts: 2.36 us -> 0.01 us
    pallas_call x1, Pallas kernels: 47.6 us -> 46.9 us  [body(): pl.pallas_call(functools.partial(kernel, count), out_shape=jax.ShapeDtype...]
where the time goes in v3:
time: 50 us; the launch traced here: 49.8 us
  Pallas kernels  46.9 us (94%)
  other arithmetic  2.85 us (6%)
    pallas_call x1, Pallas kernels, body(): pl.pallas_call(functools.partial(kernel, count), out_shape=jax.ShapeDtype...  46.9 us
    add x1, other arithmetic, body(): coupled + (alpha_energy[:, None] + beta_energy[None, :]) * coefficients  2.85 us

profile of v3, /device:TPU:2, one launch (start us, length us, event | category | flops | bytes accessed | tf_op | source)
XLA Modules:
  0.0 49.8 jit_solution(9321054900055478882)
XLA Ops:
  0.0 0.0 copy-start.1
  0.0 0.0 copy-start
  0.0 46.9 %shard_map.55 = f32[768,384]{1,0:T(8,128)} custom-call(f32[768,384]{1,0:T(8,128)} %c_hbm.1, bf16[1,3,768,768]{3,2,1,0:T(8,128)(2,1)} %h_hbm.1, s32[1,3]{1,0:T(1,128)} %cols_hbm.1), custom_call_target="tpu_custom_call" | custom-call | flops 2717908992 | bytes 4718592 | tf_op jit(solution)/shard_map/pallas_call | solution.py:230
  47.0 0.0 copy-done.1
  47.0 0.0 copy-done
  47.0 2.8 %multiply_add_fusion = f32[768,384]{1,0:T(8,128)} fusion(f32[768,384]{1,0:T(8,128)} %shard_map.55, f32[768,384]{1,0:T(8,128)} %c_hbm.1, f32[384]{0:T(512)S(1)} %copy-done.1, f32[768]{0:T(1024)S(1)} %copy-done), kind=kLoop, calls=%fused_computation | loop fusion | flops 884736 | bytes 3543552 | tf_op jit(solution)/shard_map/add | solution.py:253
Async XLA Ops:
  0.0 47.0 %copy-start.1 = (f32[384]{0:T(512)S(1)}, f32[384]{0:T(512)}, u32[]{:S(2)}) copy-start(f32[384]{0:T(512)} %param.9) | copy-start | bytes 4612
  0.0 47.0 %copy-start = (f32[768]{0:T(1024)S(1)}, f32[768]{0:T(1024)}, u32[]{:S(2)}) copy-start(f32[768]{0:T(1024)} %param.8) | copy-start | bytes 9220

commit v4 on v3

--- a/solution.py
+++ b/solution.py
@@ -119,9 +119,10 @@
             def _(i):
                 at = pl.ds(pl.multiple_of(i * quarter, quarter), quarter)
                 hb[s, at, :] = ha[slots[s], at, :]
-            for d in range(1, pairs):
-                for c in range(2):
-                    spread(s, d, c).start()
+            if s == 0:
+                for d in range(1, pairs):
+                    for c in range(2):
+                        spread(s, d, c).start()
             whole(s).start()
 
     y_wait.wait_recv()
@@ -132,6 +133,14 @@
     def _():
         start_cross()
 
+    @pl.when(source)
+    def _():
+        for s in range(1, 3):
+            for d in range(1, pairs):
+                for c in range(2):
+                    spread(s - 1, d, c).wait_send()
+                    spread(s, d, c).start()
+
     mine, theirs = 2 * (1 - side) + core, 2 * side + core
 
     @pl.when(jnp.logical_not(near))
@@ -157,10 +166,9 @@
 
     @pl.when(source)
     def _():
-        for s in range(3):
-            for d in range(1, pairs):
-                for c in range(2):
-                    spread(s, d, c).wait_send()
+        for d in range(1, pairs):
+            for c in range(2):
+                spread(2, d, c).wait_send()
 
     @pl.when(near)
     def _():

time: 50 us -> 51.8 us (1.036)
  Pallas kernels: 46.9 us -> 48.7 us
    pallas_call x1, Pallas kernels: 46.9 us -> 48.7 us  [body(): pl.pallas_call(functools.partial(kernel, count), out_shape=jax.ShapeDtype...]
where the time goes in v4:
time: 51.8 us; the launch traced here: 51.6 us
  Pallas kernels  48.7 us (94%)
  other arithmetic  2.85 us (6%)
    pallas_call x1, Pallas kernels, body(): pl.pallas_call(functools.partial(kernel, count), out_shape=jax.ShapeDtype...  48.7 us
    add x1, other arithmetic, body(): coupled + (alpha_energy[:, None] + beta_energy[None, :]) * coefficients  2.85 us

profile of v4, /device:TPU:2, one launch (start us, length us, event | category | flops | bytes accessed | tf_op | source)
XLA Modules:
  0.0 51.6 jit_solution(18281238296434274736)
XLA Ops:
  0.0 0.0 copy-start.1
  0.0 0.0 copy-start
  0.0 48.7 %shard_map.55 = f32[768,384]{1,0:T(8,128)} custom-call(f32[768,384]{1,0:T(8,128)} %c_hbm.1, bf16[1,3,768,768]{3,2,1,0:T(8,128)(2,1)} %h_hbm.1, s32[1,3]{1,0:T(1,128)} %cols_hbm.1), custom_call_target="tpu_custom_call" | custom-call | flops 2717908992 | bytes 4718592 | tf_op jit(solution)/shard_map/pallas_call | solution.py:238
  48.8 0.0 copy-done.1
  48.8 0.0 copy-done
  48.8 2.8 %multiply_add_fusion = f32[768,384]{1,0:T(8,128)} fusion(f32[768,384]{1,0:T(8,128)} %shard_map.55, f32[768,384]{1,0:T(8,128)} %c_hbm.1, f32[384]{0:T(512)S(1)} %copy-done.1, f32[768]{0:T(1024)S(1)} %copy-done), kind=kLoop, calls=%fused_computation | loop fusion | flops 884736 | bytes 3543552 | tf_op jit(solution)/shard_map/add | solution.py:261
Async XLA Ops:
  0.0 48.8 %copy-start.1 = (f32[384]{0:T(512)S(1)}, f32[384]{0:T(512)}, u32[]{:S(2)}) copy-start(f32[384]{0:T(512)} %param.9) | copy-start | bytes 4612
  0.0 48.8 %copy-start = (f32[768]{0:T(1024)S(1)}, f32[768]{0:T(1024)}, u32[]{:S(2)}) copy-start(f32[768]{0:T(1024)} %param.8) | copy-start | bytes 9220

commit v5 on v3

--- a/solution.py
+++ b/solution.py
@@ -128,7 +128,7 @@
     z_far = z_copies(1, 1 - side)
     for copy in z_far:
         copy.start()
-    @pl.when(jnp.logical_not(near))
+    @pl.when(jnp.logical_not(source))
     def _():
         start_cross()
 
@@ -162,7 +162,7 @@
                 for c in range(2):
                     spread(s, d, c).wait_send()
 
-    @pl.when(near)
+    @pl.when(source)
     def _():
         start_cross()
 

time: 50 us -> 50.5 us (1.010)
  Pallas kernels: 46.9 us -> 47.5 us
    pallas_call x1, Pallas kernels: 46.9 us -> 47.5 us  [body(): pl.pallas_call(functools.partial(kernel, count), out_shape=jax.ShapeDtype...]
where the time goes in v5:
time: 50.5 us; the launch traced here: 50.4 us
  Pallas kernels  47.5 us (94%)
  other arithmetic  2.85 us (6%)
    pallas_call x1, Pallas kernels, body(): pl.pallas_call(functools.partial(kernel, count), out_shape=jax.ShapeDtype...  47.5 us
    add x1, other arithmetic, body(): coupled + (alpha_energy[:, None] + beta_energy[None, :]) * coefficients  2.85 us

profile of v5, /device:TPU:2, one launch (start us, length us, event | category | flops | bytes accessed | tf_op | source)
XLA Modules:
  0.0 50.4 jit_solution(4023567671448720194)
XLA Ops:
  0.0 0.0 copy-start.1
  0.0 0.0 copy-start
  0.0 47.5 %shard_map.55 = f32[768,384]{1,0:T(8,128)} custom-call(f32[768,384]{1,0:T(8,128)} %c_hbm.1, bf16[1,3,768,768]{3,2,1,0:T(8,128)(2,1)} %h_hbm.1, s32[1,3]{1,0:T(1,128)} %cols_hbm.1), custom_call_target="tpu_custom_call" | custom-call | flops 2717908992 | bytes 4718592 | tf_op jit(solution)/shard_map/pallas_call | solution.py:230
  47.5 0.0 copy-done.1
  47.5 0.0 copy-done
  47.6 2.8 %multiply_add_fusion = f32[768,384]{1,0:T(8,128)} fusion(f32[768,384]{1,0:T(8,128)} %shard_map.55, f32[768,384]{1,0:T(8,128)} %c_hbm.1, f32[384]{0:T(512)S(1)} %copy-done.1, f32[768]{0:T(1024)S(1)} %copy-done), kind=kLoop, calls=%fused_computation | loop fusion | flops 884736 | bytes 3543552 | tf_op jit(solution)/shard_map/add | solution.py:253
Async XLA Ops:
  0.0 47.5 %copy-start.1 = (f32[384]{0:T(512)S(1)}, f32[384]{0:T(512)}, u32[]{:S(2)}) copy-start(f32[384]{0:T(512)} %param.9) | copy-start | bytes 4612
  0.0 47.5 %copy-start = (f32[768]{0:T(1024)S(1)}, f32[768]{0:T(1024)}, u32[]{:S(2)}) copy-start(f32[768]{0:T(1024)} %param.8) | copy-start | bytes 9220
